TPU v7x, 128 devices: a whole 4x4x4 slice. The times are simulated.
128 devices in a mesh: ctx: 16 (over x, y), ch: 8 (over z, core).
Axes of the slice: x: 4, y: 4, z: 4, core: 2. Of those that a mesh axis runs over, the one named last changes fastest.
Arguments:
- keyed_values: bfloat16 [2048, 8192], P('ctx', 'ch'), may hold values from -6 to 6
- gate_values: bfloat16 [2048, 8192], P('ctx', 'ch'), may hold values from -6 to 6
- long_filter: float32 [2048, 8192], P('ctx', 'ch'), may hold values from -0.125 to 0.125
- skip_bias: float32 [8192], P('ch'), may hold values from -1 to 1
- out_weight: bfloat16 [8192, 8192], P('ch'), may hold values from -0.09375 to 0.09375
Outputs:
- mixed: float32 [2048, 8192], P('ctx', 'ch')
All inputs are finite; a program needn't handle non-finite values.
Results may differ from a plain program's by a relative error of at most 0.023.
Values may be sent and summed in bfloat16 or wider, within the bound.
A program may use at most 128 MiB of HBM per device.

v0:
```python
import math

import jax
import jax.numpy as jnp
from jax import lax
from jax.sharding import PartitionSpec as P

HIGHEST = lax.Precision.HIGHEST
TWO_PI = 2.0 * math.pi


def from_partner(block, axis, distance):
    count = lax.axis_size(axis)
    route = []
    for low in range(count):
        high = low | 1 << distance
        if high != low and high < count:
            route += [(low, high), (high, low)]
    return lax.ppermute(block, axis, route)


def table_of(numbers, period):
    angles = (numbers % period).astype(jnp.float32) * (TWO_PI / period)
    return (jnp.cos(angles), jnp.sin(angles))


def rotate(real_part, imag_part, cosine, sine_part, direction):
    return (
        real_part * cosine - direction * imag_part * sine_part,
        imag_part * cosine + direction * real_part * sine_part,
    )


def along_rows(real_part, imag_part, extent, direction):
    indices = jnp.arange(extent, dtype=jnp.int32)
    cosine, sine_part = table_of(indices[:, None] * indices[None, :], extent)

    def contract(matrix, values):
        return jnp.einsum("kr,...rc->...kc", matrix, values, precision=HIGHEST)

    new_real = contract(cosine, real_part) - direction * contract(sine_part, imag_part)
    new_imag = contract(cosine, imag_part) + direction * contract(sine_part, real_part)
    return (new_real, new_imag)


def reversed_bits(position, level_count):
    reversed_index = jnp.zeros((), jnp.int32)
    for bit_level in range(level_count):
        digit = jnp.bitwise_and(jnp.right_shift(position, bit_level), 1)
        reversed_index = reversed_index + jnp.left_shift(digit, level_count - 1 - bit_level)
    return reversed_index


def on_device(keyed_values, gate_values, long_filter, skip_bias, out_weight):
    shard_count = lax.axis_size("ctx")
    shard_index = lax.axis_index("ctx")
    level_count = shard_count.bit_length() - 1
    row_count, channels = keyed_values.shape
    full_length = 2 * shard_count * row_count
    values32 = keyed_values.astype(jnp.float32)
    signals = jnp.stack([values32, long_filter])
    parity = jnp.arange(2, dtype=jnp.int32)
    samples = jnp.arange(row_count, dtype=jnp.int32)
    cosine, sine_part = table_of(shard_index * parity, 2 * shard_count)
    real_part = signals[:, None] * cosine[:, None, None]
    imag_part = -signals[:, None] * sine_part[:, None, None]
    carried = jnp.stack([real_part, imag_part])
    for bit_level in reversed(range(level_count)):
        stride = 1 << bit_level
        partner = from_partner(carried.astype(jnp.bfloat16), "ctx", bit_level).astype(carried.dtype)
        is_upper = jnp.bitwise_and(jnp.right_shift(shard_index, bit_level), 1) == 1
        cosine, sine_part = table_of(shard_index % stride, 2 * stride)
        diff_real, diff_imag = rotate(
            partner[0] - carried[0], partner[1] - carried[1], cosine, sine_part, -1.0
        )
        carried = jnp.where(is_upper, jnp.stack([diff_real, diff_imag]), carried + partner)
    owner_index = reversed_bits(shard_index, level_count)
    cosine, sine_part = table_of(
        (2 * owner_index + parity)[:, None] * samples[None, :], full_length
    )
    real_part, imag_part = rotate(
        carried[0], carried[1], cosine[:, :, None], sine_part[:, :, None], -1.0
    )
    spec_real, spec_imag = along_rows(real_part, imag_part, row_count, -1.0)
    prod_real = spec_real[0] * spec_real[1] - spec_imag[0] * spec_imag[1]
    prod_imag = spec_real[0] * spec_imag[1] + spec_imag[0] * spec_real[1]
    back_real, back_imag = along_rows(prod_real, prod_imag, row_count, 1.0)
    cosine, sine_part = table_of(
        (2 * owner_index + parity)[:, None] * samples[None, :], full_length
    )
    back_real, back_imag = rotate(
        back_real, back_imag, cosine[:, :, None], sine_part[:, :, None], 1.0
    )
    carried = jnp.stack([back_real, back_imag])
    for bit_level in range(level_count):
        stride = 1 << bit_level
        partner = from_partner(carried.astype(jnp.bfloat16), "ctx", bit_level).astype(carried.dtype)
        is_upper = jnp.bitwise_and(jnp.right_shift(shard_index, bit_level), 1) == 1
        lower_side = jnp.where(is_upper, partner, carried)
        upper_side = jnp.where(is_upper, carried, partner)
        cosine, sine_part = table_of(shard_index % stride, 2 * stride)
        turned = jnp.stack(rotate(upper_side[0], upper_side[1], cosine, sine_part, 1.0))
        carried = jnp.where(is_upper, lower_side - turned, lower_side + turned)
    cosine, sine_part = table_of(shard_index, 2 * shard_count)
    convolved = carried[0, 0] + carried[0, 1] * cosine - carried[1, 1] * sine_part
    convolved = convolved / full_length
    gated_rows = ((convolved + skip_bias * values32) * gate_values.astype(jnp.float32)).astype(
        jnp.bfloat16
    )
    partial_value = jnp.dot(gated_rows, out_weight, preferred_element_type=jnp.float32)
    return lax.psum_scatter(
        partial_value.astype(jnp.bfloat16), "ch", scatter_dimension=1, tiled=True
    ).astype(jnp.float32)


def solution(mesh):
    return jax.shard_map(
        on_device,
        mesh=mesh,
        in_specs=(P("ctx", "ch"), P("ctx", "ch"), P("ctx", "ch"), P("ch"), P("ch", None)),
        out_specs=P("ctx", "ch"),
        check_vma=False,
    )
```

profile of v0, /device:TPU:1, one launch (start us, length us, event | category | flops | bytes accessed | tf_op | source)
XLA Modules:
  0.0 376.0 jit_solution(8319903564538979958)
XLA Ops:
  7.8 1.2 copy.7
  10.3 1.9 fusion
  12.3 3.6 collective-permute-start
  16.0 45.0 %collective-permute-done = bf16[2,2,2,128,1024]{3,4,2,1,0:T(8,128)(2,1)} collective-permute-done((bf16[2,2,2,128,1024]{3,4,2,1,0:T(8,128)(2,1)}, bf16[2,2,2,128,1024]{3,4,2,1,0:T(8,128)(2,1)}, u32[]{:S(2)}, u32[]{:S(2)}) %collective-permute-start) | collective-permute-done | bytes 2097184 | tf_op jit(solution)/shard_map/ppermute | solution.py:19
  61.1 1.9 convert_element_type.129
  64.5 4.2 %fusion.95 = (bf16[2,2,2,128,1024]{3,4,2,1,0:T(8,128)(2,1)}, f32[2,2,2,128,1024]{3,4,2,1,0:T(8,128)}) fusion(bf16[2,2,2,128,1024]{3,4,2,1,0:T(8,128)(2,1)} %collective-permute-done, f32[1,2,2,128,1024]{3,4,2,1,0:T(8,128)S(1)} %broadcast_multiply_fusion, f32[1,2,2,128,1024]{3,4,2,1,0:T(8,128)S(1)} %copy-done.4, ...), kind=kLoop, calls=%fused_computation.163 | loop fusion | flops 6291456 | bytes 16777216 | tf_op jit(solution)/shard_map/convert_element_type | solution.py:70
  68.8 1.6 collective-permute-start.1
  70.5 44.1 %collective-permute-done.1 = bf16[2,2,2,128,1024]{3,4,2,1,0:T(8,128)(2,1)S(1)} collective-permute-done((bf16[2,2,2,128,1024]{3,4,2,1,0:T(8,128)(2,1)}, bf16[2,2,2,128,1024]{3,4,2,1,0:T(8,128)(2,1)S(1)}, u32[]{:S(2)}, u32[]{:S(2)}) %collective-permute-start.1) | collective-permute-done | bytes 2097184 | tf_op jit(solution)/shard_map/ppermute | solution.py:19
  115.7 3.5 fusion.94
  119.2 3.2 collective-permute-start.2
  122.6 43.4 %collective-permute-done.2 = bf16[2,2,2,128,1024]{3,4,2,1,0:T(8,128)(2,1)S(1)} collective-permute-done((bf16[2,2,2,128,1024]{3,4,2,1,0:T(8,128)(2,1)}, bf16[2,2,2,128,1024]{3,4,2,1,0:T(8,128)(2,1)S(1)}, u32[]{:S(2)}, u32[]{:S(2)}) %collective-permute-start.2) | collective-permute-done | bytes 2097184 | tf_op jit(solution)/shard_map/ppermute | solution.py:19
  167.0 3.5 fusion.93
  171.8 42.9 %collective-permute-done.3 = bf16[2,2,2,128,1024]{3,4,2,1,0:T(8,128)(2,1)S(1)} collective-permute-done((bf16[2,2,2,128,1024]{3,4,2,1,0:T(8,128)(2,1)}, bf16[2,2,2,128,1024]{3,4,2,1,0:T(8,128)(2,1)S(1)}, u32[]{:S(2)}, u32[]{:S(2)}) %collective-permute-start.3) | collective-permute-done | bytes 2097184 | tf_op jit(solution)/shard_map/ppermute | solution.py:19
  216.0 2.1 fusion.16
  218.2 2.1 fusion.15
  220.4 2.2 subtract_bitcast_fusion
  222.5 2.2 add_bitcast_fusion
  225.0 1.2 fusion.2
  226.2 1.5 fusion.6
  227.7 1.3 convolution_add_fusion
  228.9 1.4 subtract_bitcast_fusion.1
  231.5 19.6 %collective-permute-done.4 = bf16[2,2,128,1024]{2,3,1,0:T(8,128)(2,1)S(1)} collective-permute-done((bf16[2,2,128,1024]{2,3,1,0:T(8,128)(2,1)S(1)}, bf16[2,2,128,1024]{2,3,1,0:T(8,128)(2,1)S(1)}, u32[]{:S(2)}, u32[]{:S(2)}) %collective-permute-start.4) | collective-permute-done | bytes 1048608 | tf_op jit(solution)/shard_map/ppermute | solution.py:19
  251.8 2.5 collective-permute-start.5
  254.3 22.1 %collective-permute-done.5 = bf16[2,2,128,1024]{2,3,1,0:T(8,128)(2,1)S(1)} collective-permute-done((bf16[2,2,128,1024]{2,3,1,0:T(8,128)(2,1)S(1)}, bf16[2,2,128,1024]{2,3,1,0:T(8,128)(2,1)S(1)}, u32[]{:S(2)}, u32[]{:S(2)}) %collective-permute-start.5) | collective-permute-done | bytes 1048608 | tf_op jit(solution)/shard_map/ppermute | solution.py:19
  278.3 19.4 %collective-permute-done.6 = bf16[2,2,128,1024]{2,3,1,0:T(8,128)(2,1)S(1)} collective-permute-done((bf16[2,2,128,1024]{2,3,1,0:T(8,128)(2,1)S(1)}, bf16[2,2,128,1024]{2,3,1,0:T(8,128)(2,1)S(1)}, u32[]{:S(2)}, u32[]{:S(2)}) %collective-permute-start.6) | collective-permute-done | bytes 1048608 | tf_op jit(solution)/shard_map/ppermute | solution.py:19
  298.1 1.4 fusion.90
  299.4 2.3 collective-permute-start.7
  301.9 1.8 copy.8
  303.7 18.1 %collective-permute-done.7 = bf16[2,2,128,1024]{2,3,1,0:T(8,128)(2,1)S(1)} collective-permute-done((bf16[2,2,128,1024]{2,3,1,0:T(8,128)(2,1)}, bf16[2,2,128,1024]{2,3,1,0:T(8,128)(2,1)S(1)}, u32[]{:S(2)}, u32[]{:S(2)}) %collective-permute-start.7) | collective-permute-done | bytes 1048608 | tf_op jit(solution)/shard_map/ppermute | solution.py:19
  323.1 9.8 %convolution_convert_fusion = bf16[128,8192]{1,0:T(8,128)(2,1)} fusion(bf16[1024,8192]{1,0:T(8,128)(2,1)} %param.9, bf16[128,1024]{0,1:T(8,128)(2,1)S(1)} %copy.6, f32[2,2,128,1024]{2,3,1,0:T(8,128)S(1)} %add_select_fusion, bf16[128,1024]{0,1:T(8,128)(2,1)S(1)} %copy-done.7, f32[1024]{0:T(1024)S(1)} %copy-done.8, f32[]{:T(128)S(6)} %sin.52, f32[]{:T(128)S(6)} %cos.52), kind=kOutput, calls=%fused_computation | convolution fusion | flops 2149974016 | bytes 20975624 | tf_op jit(solution)/shard_map/dot_general | solution.py:110
  332.9 34.4 %reduce-scatter.2.cloned.1.call-done = bf16[128,1024]{1,0:T(8,128)(2,1)} async-done(((bf16[128,8192]{1,0:T(8,128)(2,1)}), bf16[128,1024]{1,0:T(8,128)(2,1)}) %reduce-scatter.2.cloned.1.call-update) | async-done | bytes 262160 | tf_op jit(solution)/shard_map/reduce_scatter | solution.py:111
  367.4 1.8 convert_element_type.153
  (52 shorter events, 14.6 us)
Async XLA Ops:
  6.5 360.8 %reduce-scatter.2.cloned.1.call-start = ((), (), s32[]{:S(2)}) async-start(), calls=%async_computation.1 | async-start | bytes 2359296 | tf_op jit(solution)/shard_map/reduce_scatter | solution.py:111
  9.1 1.0 copy-start.5
  10.3 2.0 copy-start.3
  12.3 48.8 %collective-permute-start = (bf16[2,2,2,128,1024]{3,4,2,1,0:T(8,128)(2,1)}, bf16[2,2,2,128,1024]{3,4,2,1,0:T(8,128)(2,1)}, u32[]{:S(2)}, u32[]{:S(2)}) collective-permute-start(bf16[2,2,2,128,1024]{3,4,2,1,0:T(8,128)(2,1)} %fusion), channel_id=1, source_target_pairs={{0,64},{64,0},{8,72},{72,8},{16,80},{80,16},{24,88},{88,24},{32,96... | collective-permute-start | bytes 6291464 | tf_op jit(solution)/shard_map/ppermute | solution.py:19
  16.0 46.9 %copy-start.6 = (f32[2,128,1024]{1,2,0:T(8,128)S(1)}, f32[2,128,1024]{1,2,0:T(8,128)}, u32[]{:S(2)}) copy-start(f32[2,128,1024]{1,2,0:T(8,128)} %copy-done.5) | copy-start | bytes 3145732
  62.9 1.6 copy-start.4
  68.8 45.9 %collective-permute-start.1 = (bf16[2,2,2,128,1024]{3,4,2,1,0:T(8,128)(2,1)}, bf16[2,2,2,128,1024]{3,4,2,1,0:T(8,128)(2,1)S(1)}, u32[]{:S(2)}, u32[]{:S(2)}) collective-permute-start(bf16[2,2,2,128,1024]{3,4,2,1,0:T(8,128)(2,1)} %get-tuple-element.15), channel_id=1, source_target_pairs={{0,32},{32,0},{8,40},{40,8},{16,48},{48,16},{24,56},{56,24},{64,96... | collective-permute-start | bytes 6291464 | tf_op jit(solution)/shard_map/ppermute | solution.py:19
  70.5 44.4 %copy-start = (f32[2,2,2,128,1024]{3,4,2,1,0:T(8,128)S(1)}, f32[2,2,2,128,1024]{3,4,2,1,0:T(8,128)}, u32[]{:S(2)}) copy-start(f32[2,2,2,128,1024]{3,4,2,1,0:T(8,128)} %get-tuple-element.16) | copy-start | bytes 12582916
  119.2 46.8 %collective-permute-start.2 = (bf16[2,2,2,128,1024]{3,4,2,1,0:T(8,128)(2,1)}, bf16[2,2,2,128,1024]{3,4,2,1,0:T(8,128)(2,1)S(1)}, u32[]{:S(2)}, u32[]{:S(2)}) collective-permute-start(bf16[2,2,2,128,1024]{3,4,2,1,0:T(8,128)(2,1)} %get-tuple-element.13), channel_id=1, source_target_pairs={{0,16},{16,0},{8,24},{24,8},{32,48},{48,32},{40,56},{56,40},{64,80... | collective-permute-start | bytes 6291464 | tf_op jit(solution)/shard_map/ppermute | solution.py:19
  122.5 43.7 %copy-start.1 = (f32[2,2,2,128,1024]{3,4,2,1,0:T(8,128)S(1)}, f32[2,2,2,128,1024]{3,4,2,1,0:T(8,128)}, u32[]{:S(2)}) copy-start(f32[2,2,2,128,1024]{3,4,2,1,0:T(8,128)} %get-tuple-element.14) | copy-start | bytes 12582916
  170.5 44.1 %collective-permute-start.3 = (bf16[2,2,2,128,1024]{3,4,2,1,0:T(8,128)(2,1)}, bf16[2,2,2,128,1024]{3,4,2,1,0:T(8,128)(2,1)S(1)}, u32[]{:S(2)}, u32[]{:S(2)}) collective-permute-start(bf16[2,2,2,128,1024]{3,4,2,1,0:T(8,128)(2,1)} %get-tuple-element.11), channel_id=1, source_target_pairs={{0,8},{8,0},{16,24},{24,16},{32,40},{40,32},{48,56},{56,48},{64,72... | collective-permute-start | bytes 6291464 | tf_op jit(solution)/shard_map/ppermute | solution.py:19
  171.8 43.1 %copy-start.2 = (f32[2,2,2,128,1024]{3,4,2,1,0:T(8,128)S(1)}, f32[2,2,2,128,1024]{3,4,2,1,0:T(8,128)}, u32[]{:S(2)}) copy-start(f32[2,2,2,128,1024]{3,4,2,1,0:T(8,128)} %get-tuple-element.12) | copy-start | bytes 12582916
  230.5 20.6 %collective-permute-start.4 = (bf16[2,2,128,1024]{2,3,1,0:T(8,128)(2,1)S(1)}, bf16[2,2,128,1024]{2,3,1,0:T(8,128)(2,1)S(1)}, u32[]{:S(2)}, u32[]{:S(2)}) collective-permute-start(bf16[2,2,128,1024]{2,3,1,0:T(8,128)(2,1)S(1)} %fusion.1), channel_id=1, source_target_pairs={{0,8},{8,0},{16,24},{24,16},{32,40},{40,32},{48,56},{56,48},{64,72... | collective-permute-start | bytes 3145736 | tf_op jit(solution)/shard_map/ppermute | solution.py:19
  251.8 24.6 %collective-permute-start.5 = (bf16[2,2,128,1024]{2,3,1,0:T(8,128)(2,1)S(1)}, bf16[2,2,128,1024]{2,3,1,0:T(8,128)(2,1)S(1)}, u32[]{:S(2)}, u32[]{:S(2)}) collective-permute-start(bf16[2,2,128,1024]{2,3,1,0:T(8,128)(2,1)S(1)} %get-tuple-element.9), channel_id=1, source_target_pairs={{0,16},{16,0},{8,24},{24,8},{32,48},{48,32},{40,56},{56,40},{64,80... | collective-permute-start | bytes 3145736 | tf_op jit(solution)/shard_map/ppermute | solution.py:19
  277.2 20.4 %collective-permute-start.6 = (bf16[2,2,128,1024]{2,3,1,0:T(8,128)(2,1)S(1)}, bf16[2,2,128,1024]{2,3,1,0:T(8,128)(2,1)S(1)}, u32[]{:S(2)}, u32[]{:S(2)}) collective-permute-start(bf16[2,2,128,1024]{2,3,1,0:T(8,128)(2,1)S(1)} %get-tuple-element.7), channel_id=1, source_target_pairs={{0,32},{32,0},{8,40},{40,8},{16,48},{48,16},{24,56},{56,24},{64,96... | collective-permute-start | bytes 3145736 | tf_op jit(solution)/shard_map/ppermute | solution.py:19
  299.4 22.3 %collective-permute-start.7 = (bf16[2,2,128,1024]{2,3,1,0:T(8,128)(2,1)}, bf16[2,2,128,1024]{2,3,1,0:T(8,128)(2,1)S(1)}, u32[]{:S(2)}, u32[]{:S(2)}) collective-permute-start(bf16[2,2,128,1024]{2,3,1,0:T(8,128)(2,1)} %get-tuple-element.5), channel_id=1, source_target_pairs={{0,64},{64,0},{8,72},{72,8},{16,80},{80,16},{24,88},{88,24},{32,96... | collective-permute-start | bytes 3145736 | tf_op jit(solution)/shard_map/ppermute | solution.py:19
  322.1 1.0 copy-start.7
  322.2 0.9 copy-start.8
Sparse Core Ops, SparseCore 0:
  333.0 34.2 reduce-scatter.1
where the time goes:
time: 379 us; the launch traced here: 376 us
  waiting for transfers between devices  289 us (76%)
  other arithmetic  26.2 us (7%)
  matrix products  23.8 us (6%)
  starting transfers between devices  16.4 us (4%)
  between operations  14.4 us (4%)
  local copies, waits for them, and re-layouts  6.27 us (2%)
    ppermute x8, waiting for transfers between devices, from_partner(): return lax.ppermute(block, axis, route)  254 us
    reduce_scatter x1, waiting for transfers between devices, on_device(): lax.psum_scatter(partial_value.astype(jnp.bfloat16), 'ch', scatter_dimens...  34.4 us
    ppermute x8, starting transfers between devices, from_partner(): return lax.ppermute(block, axis, route)  16.4 us
    convert_element_type x8, other arithmetic, on_device(): carried.astype(jnp.bfloat16)  15.4 us
    dot_general x8, matrix products, contract(): return jnp.einsum('kr,...rc->...kc', matrix, values, precision=HIGHEST)  14 us
    dot_general x1, matrix products, on_device(): jnp.dot(gated_rows, out_weight, preferred_element_type=jnp.float32)  9.78 us
  transfers between devices with their start and end apart: 9, of which 9 were waited for; matrix products, arithmetic and copies ran while one was open for 1% of the time, Pallas kernels for 0%

commit v1 on v0

v1 whole, which is shorter than its diff:
```python
import functools
import math

import jax
import jax.numpy as jnp
import ml_dtypes
import numpy as np
from jax import lax
from jax.experimental import pallas as pl
from jax.experimental.pallas import tpu as pltpu
from jax.sharding import PartitionSpec as P

MESH = pl.DeviceIdType.MESH
SIDE = 4
BLOCKS = 16
ROWS = 128
LANES = 128
HALF = 64
FULL = 2 * BLOCKS * ROWS
GROUP = 16
ROUTES = ((2, 2), (2, 1), (1, 2), (2, 3), (3, 2), (2, 0), (0, 2), (1, 1), (3, 3), (1, 3), (3, 1),
          (1, 0), (3, 0), (0, 1), (0, 3))


@functools.cache
def tables():
    a = np.arange(BLOCKS)
    forward = np.zeros((16, 2, BLOCKS))
    inverse = np.zeros((BLOCKS, 16, 2))
    for k1 in range(16):
        angle = 2 * math.pi * a * k1 / 32
        forward[k1, 0] = np.cos(angle)
        forward[k1, 1] = -np.sin(angle)
        inverse[:, k1, 0] = 2 * np.cos(angle)
        inverse[:, k1, 1] = -2 * np.sin(angle)
    forward[0, 1] = (-1.0) ** a
    inverse[:, 0, 0] = 1.0
    inverse[:, 0, 1] = (-1.0) ** a
    eye = np.eye(GROUP)
    first = np.kron(forward.reshape(32, BLOCKS), eye)
    last = np.kron(inverse.reshape(BLOCKS, 32) / 32, eye)
    b = np.arange(ROWS)
    middle = np.zeros((16, 256, 256))
    middle_back = np.zeros((16, 256, 256))
    for k1 in range(1, 16):
        angle = 2 * math.pi * np.outer(k1 + 32 * b, b) / FULL
        c, s = np.cos(angle), np.sin(angle)
        middle[k1] = np.block([[c, s], [-s, c]])
        middle_back[k1] = np.block([[c.T, -s.T], [s.T, c.T]]) / 128
    k2 = np.arange(64)
    angle = 2 * math.pi * np.outer(k2, b) / 128
    c, s = np.cos(angle), np.sin(angle)
    imag = -s
    imag[0] = (-1.0) ** b
    middle[0, 0:64, 0:128] = c
    middle[0, 128:192, 0:128] = imag
    weight = np.full((64, 1), 2.0)
    weight[0] = 1.0
    middle_back[0, 0:128, 0:64] = (weight * c).T / 128
    middle_back[0, 0:128, 128:192] = (weight * imag).T / 128
    angle = 2 * math.pi * np.outer(16 + 32 * k2, b) / FULL
    c, s = np.cos(angle), np.sin(angle)
    middle[0, 64:128, 128:256] = c
    middle[0, 192:256, 128:256] = -s
    middle_back[0, 128:256, 64:128] = 2 * c.T / 128
    middle_back[0, 128:256, 192:256] = -2 * s.T / 128
    return tuple(t.astype(ml_dtypes.bfloat16) for t in (first, middle, middle_back, last))


def dot(left, right):
    return jnp.dot(left, right, preferred_element_type=jnp.float32)


def kernel(v_hbm, g_hbm, h_hbm, bias_ref, w_hbm, f1_hbm, m_hbm, mb_hbm, f2_hbm, out_ref,
           v, g, h, w, f1, m, mb, f2, send, recv, mid, back, bsend, brecv, gated, psend, precv, ring_s, ring_r,
           keep, in_sem, w_sem, s_sem, r_sem, bs_sem, br_sem, ps_sem, pr_sem, rs_sem, rr_sem):
    ctx, ch = lax.axis_index("ctx"), lax.axis_index("ch")
    x, y = ctx // SIDE, lax.rem(ctx, SIDE)
    z, core = ch // 2, lax.rem(ch, 2)

    def shifted(position, by):
        return lax.rem(position + by, SIDE)

    partners = [shifted(x, dx) * SIDE + shifted(y, dy) for dx, dy in ROUTES]
    other = (ctx, z * 2 + 1 - core)
    up = (ctx, shifted(z, 1) * 2 + core)
    down = (ctx, shifted(z, 3) * 2 + core)

    barrier = pltpu.get_barrier_semaphore()
    for partner in partners:
        pl.semaphore_signal(barrier, inc=1, device_id=(partner, ch), device_id_type=MESH)
    for device in (other, up, down):
        pl.semaphore_signal(barrier, inc=1, device_id=device, device_id_type=MESH)

    loads = []
    for i, (src, dst) in enumerate(((h_hbm, h), (v_hbm, v), (f1_hbm, f1), (m_hbm, m), (mb_hbm, mb), (f2_hbm, f2), (g_hbm, g))):
        load = pltpu.make_async_copy(src, dst, in_sem.at[i])
        load.start()
        loads.append(load)
    w_load = pltpu.make_async_copy(w_hbm, w, w_sem)
    w_load.start()

    low = lax.broadcasted_iota(jnp.int32, (ROWS, LANES), 1) < HALF
    loads[0].wait()
    loads[1].wait()
    for t in range(8):
        columns = slice(t * LANES, (t + 1) * LANES)
        values, taps = v[:, columns].astype(jnp.float32), h[:, columns]
        send[2 * t] = jnp.where(low, values, pltpu.roll(taps, HALF, 1)).astype(jnp.bfloat16)
        send[2 * t + 1] = jnp.where(low, pltpu.roll(values, HALF, 1), taps).astype(jnp.bfloat16)

    pl.semaphore_wait(barrier, len(ROUTES) + 3)
    copies = []
    for i, partner in enumerate(partners):
        copy = pltpu.make_async_remote_copy(
            send.at[partner], recv.at[ctx], s_sem.at[i], r_sem.at[i], device_id=(partner, ch), device_id_type=MESH)
        copy.start()
        copies.append(copy)
    recv[ctx] = send[ctx]
    for i in range(2, 6):
        loads[i].wait()
    for copy in copies:
        copy.wait()

    for k in range(ROWS // GROUP):
        rows = slice(k * GROUP, (k + 1) * GROUP)
        part = dot(f1[...], recv[:, rows, :].reshape(BLOCKS * GROUP, LANES))
        mid[:, :, rows, :] = part.astype(jnp.bfloat16).reshape(16, 2, GROUP, LANES)
    low_half = lax.broadcasted_iota(jnp.int32, (HALF, LANES), 1) < HALF
    for s in range(16):
        spectrum = dot(m[s], mid[s].reshape(2 * ROWS, LANES))
        real, imag = spectrum[:ROWS], spectrum[ROWS:]
        real2, imag2 = pltpu.roll(real, HALF, 1), pltpu.roll(imag, HALF, 1)
        rr, ii = real * real2, imag * imag2
        prod_real, prod_imag = rr - ii, real * imag2 + imag * real2
        if s == 0:
            top = lax.broadcasted_iota(jnp.int32, (ROWS, LANES), 0) == 0
            prod_real, prod_imag = jnp.where(top, rr, prod_real), jnp.where(top, ii, prod_imag)
        product = jnp.concatenate([prod_real, prod_imag], axis=0).astype(jnp.bfloat16)
        turned = dot(mb[s], product)
        for part in range(2):
            first, second = turned[part * ROWS:part * ROWS + HALF], turned[part * ROWS + HALF:(part + 1) * ROWS]
            back[s, part] = jnp.where(low_half, first, second).astype(jnp.bfloat16)
    for k in range(HALF // GROUP):
        rows = slice(k * GROUP, (k + 1) * GROUP)
        part = dot(f2[...], back[:, :, rows, :].reshape(2 * 16 * GROUP, LANES))
        bsend[:, rows, :] = part.astype(jnp.bfloat16).reshape(BLOCKS, GROUP, LANES)

    copies = []
    for i, partner in enumerate(partners):
        copy = pltpu.make_async_remote_copy(
            bsend.at[partner], brecv.at[ctx], bs_sem.at[i], br_sem.at[i], device_id=(partner, ch), device_id_type=MESH)
        copy.start()
        copies.append(copy)
    brecv[ctx] = bsend[ctx]
    loads[6].wait()
    for copy in copies:
        copy.wait()

    for t in range(8):
        columns = slice(t * LANES, (t + 1) * LANES)
        even, odd = brecv[2 * t].astype(jnp.float32), brecv[2 * t + 1].astype(jnp.float32)
        for part in range(2):
            rows = slice(part * HALF, (part + 1) * HALF)
            if part == 0:
                convolved = jnp.where(low_half, even, pltpu.roll(odd, HALF, 1))
            else:
                convolved = jnp.where(low_half, pltpu.roll(even, HALF, 1), odd)
            values = v[rows, columns].astype(jnp.float32)
            gate = g[rows, columns].astype(jnp.float32)
            gated[rows, columns] = ((convolved + bias_ref[0:1, columns] * values) * gate).astype(jnp.bfloat16)

    w_load.wait()

    def project(distance, part, to_core):
        start = (shifted(z, distance) * 2 + to_core) * 1024 + part * 512
        return dot(gated[...], w[:, pl.ds(pl.multiple_of(start, 512), 512)])

    def to_other(distance, part):
        i = 2 * distance + part
        psend[i] = project(distance, part, 1 - core).astype(jnp.bfloat16)
        copy = pltpu.make_async_remote_copy(
            psend.at[i], precv.at[i], ps_sem.at[i], pr_sem.at[i], device_id=other, device_id_type=MESH)
        copy.start()
        return copy

    def ring(i, device):
        copy = pltpu.make_async_remote_copy(
            ring_s.at[i], ring_r.at[i], rs_sem.at[i], rr_sem.at[i], device_id=device, device_id_type=MESH)
        copy.start()
        return copy

    pair = {}
    rings = {}

    def pair_sum(distance, part):
        own = project(distance, part, core)
        pair[distance, part].wait_recv()
        return own + precv[2 * distance + part].astype(jnp.float32)

    for part in range(2):
        pair[2, part] = to_other(2, part)
    for part, device in ((0, up), (1, down)):
        ring_s[part] = pair_sum(2, part).astype(jnp.bfloat16)
        rings[part] = ring(part, device)
    pair[1, 1], pair[3, 0] = to_other(1, 1), to_other(3, 0)
    ring_s[2] = pair_sum(1, 1).astype(jnp.bfloat16)
    rings[2] = ring(2, up)
    ring_s[3] = pair_sum(3, 0).astype(jnp.bfloat16)
    rings[3] = ring(3, down)
    pair[1, 0], pair[3, 1] = to_other(1, 0), to_other(3, 1)
    for i, (distance, part, device) in ((4, (1, 0, up)), (5, (3, 1, down))):
        total = pair_sum(distance, part)
        rings[i - 4].wait_recv()
        ring_s[i] = (total + ring_r[i - 4].astype(jnp.float32)).astype(jnp.bfloat16)
        rings[i] = ring(i, device)
    for part in range(2):
        pair[0, part] = to_other(0, part)
    for part in range(2):
        keep[part] = pair_sum(0, part)
    for i in (2, 3):
        rings[i].wait_recv()
    rings[4].wait_recv()
    out_ref[:, 0:512] = keep[0] + (ring_r[4].astype(jnp.float32) + ring_r[3].astype(jnp.float32))
    rings[5].wait_recv()
    out_ref[:, 512:1024] = keep[1] + (ring_r[2].astype(jnp.float32) + ring_r[5].astype(jnp.float32))
    for copy in (*pair.values(), *rings.values()):
        copy.wait_send()


def on_device(keyed_values, gate_values, long_filter, skip_bias, out_weight):
    first, middle, middle_back, last = (jnp.asarray(t) for t in tables())
    bf, f32 = jnp.bfloat16, jnp.float32
    hbm = pl.BlockSpec(memory_space=pl.ANY)
    vmem = pl.BlockSpec(memory_space=pltpu.VMEM)
    dma = pltpu.SemaphoreType.DMA
    hops = len(ROUTES)
    return pl.pallas_call(
        kernel,
        out_shape=jax.ShapeDtypeStruct((ROWS, 1024), f32),
        in_specs=[hbm, hbm, hbm, vmem, hbm, hbm, hbm, hbm, hbm],
        out_specs=vmem,
        scratch_shapes=[
            pltpu.VMEM((ROWS, 1024), bf),
            pltpu.VMEM((ROWS, 1024), bf),
            pltpu.VMEM((ROWS, 1024), f32),
            pltpu.VMEM((1024, 8192), bf),
            pltpu.VMEM((512, 256), bf),
            pltpu.VMEM((16, 256, 256), bf),
            pltpu.VMEM((16, 256, 256), bf),
            pltpu.VMEM((256, 512), bf),
            pltpu.VMEM((BLOCKS, ROWS, LANES), bf),
            pltpu.VMEM((BLOCKS, ROWS, LANES), bf),
            pltpu.VMEM((16, 2, ROWS, LANES), bf),
            pltpu.VMEM((16, 2, HALF, LANES), bf),
            pltpu.VMEM((BLOCKS, HALF, LANES), bf),
            pltpu.VMEM((BLOCKS, HALF, LANES), bf),
            pltpu.VMEM((ROWS, 1024), bf),
            pltpu.VMEM((8, ROWS, 512), bf),
            pltpu.VMEM((8, ROWS, 512), bf),
            pltpu.VMEM((6, ROWS, 512), bf),
            pltpu.VMEM((6, ROWS, 512), bf),
            pltpu.VMEM((2, ROWS, 512), f32),
            dma((7,)),
            dma,
            dma((hops,)),
            dma((hops,)),
            dma((hops,)),
            dma((hops,)),
            dma((8,)),
            dma((8,)),
            dma((6,)),
            dma((6,)),
        ],
        compiler_params=pltpu.CompilerParams(
            collective_id=0, has_side_effects=True, vmem_limit_bytes=48 << 20),
        cost_estimate=pl.CostEstimate(flops=3 << 30, bytes_accessed=24 << 20, transcendentals=0),
    )(keyed_values, gate_values, long_filter, skip_bias.reshape(1, 1024), out_weight, first, middle, middle_back, last)


def solution(mesh):
    return jax.shard_map(
        on_device,
        mesh=mesh,
        in_specs=(P("ctx", "ch"), P("ctx", "ch"), P("ctx", "ch"), P("ch"), P("ch", None)),
        out_specs=P("ctx", "ch"),
        check_vma=False,
    )
```

time: 379 us -> 46.4 us (0.12)
  waiting for transfers between devices: 289 us -> 0 us
  Pallas kernels: 0 us -> 38.2 us
  other arithmetic: 26.2 us -> 0 us
  matrix products: 23.8 us -> 0 us
  starting transfers between devices: 16.4 us -> 0 us
  between operations: 14.4 us -> 0.02 us
    ppermute x8 -> x0, waiting for transfers between devices: 254 us -> none  [from_partner(): return lax.ppermute(block, axis, route)]
    pallas_call x0 -> x1, Pallas kernels: none -> 38.2 us  [on_device(): pl.pallas_call(kernel, out_shape=jax.ShapeDtypeStruct((ROWS, 1024), f32),...]
    reduce_scatter x1 -> x0, waiting for transfers between devices: 34.4 us -> none  [on_device(): lax.psum_scatter(partial_value.astype(jnp.bfloat16), 'ch', scatter_dimens...]
    dot_general x9 -> x0, matrix products: 23.8 us -> none  [the longest x8 14 us: contract(): return jnp.einsum('kr,...rc->...kc', matrix, values, precision=HIGHEST)]
    convert_element_type x13 -> x0, other arithmetic: 19.9 us -> none  [the longest x8 15.4 us: on_device(): carried.astype(jnp.bfloat16)]
    ppermute x8 -> x0, starting transfers between devices: 16.4 us -> none  [from_partner(): return lax.ppermute(block, axis, route)]
    unnamed x21 -> x15, local copies, waits for them, and re-layouts: 6.27 us -> 7.91 us
  transfers between devices with their start and end apart: 9 -> 0, of which waited for: 9 -> 0; matrix products, arithmetic and copies ran while one was open for 1% -> 0% of each run, Pallas kernels for 0% -> 0%
where the time goes in v1:
time: 46.4 us; the launch traced here: 46.1 us
  Pallas kernels  38.2 us (82%)
  local copies, waits for them, and re-layouts  7.91 us (17%)
    pallas_call x1, Pallas kernels, on_device(): pl.pallas_call(kernel, out_shape=jax.ShapeDtypeStruct((ROWS, 1024), f32),...  38.2 us
    unnamed x15, local copies, waits for them, and re-layouts  7.91 us

profile of v1, /device:TPU:1, one launch (start us, length us, event | category | flops | bytes accessed | tf_op | source)
XLA Modules:
  0.0 46.1 jit_solution(36859603242163928)
XLA Ops:
  0.0 0.0 copy-start
  0.0 1.6 %copy-done = bf16[16,256,256]{2,1,0:T(8,128)(2,1)S(1)} copy-done((bf16[16,256,256]{2,1,0:T(8,128)(2,1)S(1)}, bf16[16,256,256]{2,1,0:T(8,128)(2,1)}, u32[]{:S(2)}) %copy-start) | copy-done | bytes 2097176
  1.6 0.0 copy-start.1
  1.6 1.0 %copy-done.1 = f32[128,1024]{1,0:T(8,128)S(1)} copy-done((f32[128,1024]{1,0:T(8,128)S(1)}, f32[128,1024]{1,0:T(8,128)}, u32[]{:S(2)}) %copy-start.1) | copy-done | bytes 524312
  2.6 0.0 copy-start.2
  2.6 0.9 %copy-done.2 = bf16[128,1024]{1,0:T(8,128)(2,1)S(1)} copy-done((bf16[128,1024]{1,0:T(8,128)(2,1)S(1)}, bf16[128,1024]{1,0:T(8,128)(2,1)}, u32[]{:S(2)}) %copy-start.2) | copy-done | bytes 262168
  3.6 0.0 copy-start.3
  3.6 0.9 %copy-done.3 = bf16[128,1024]{1,0:T(8,128)(2,1)S(1)} copy-done((bf16[128,1024]{1,0:T(8,128)(2,1)S(1)}, bf16[128,1024]{1,0:T(8,128)(2,1)}, u32[]{:S(2)}) %copy-start.3) | copy-done | bytes 262168
  4.5 0.0 copy-start.4
  4.5 0.9 %copy-done.4 = bf16[256,512]{1,0:T(8,128)(2,1)S(1)} copy-done((bf16[256,512]{1,0:T(8,128)(2,1)S(1)}, bf16[256,512]{1,0:T(8,128)(2,1)}, u32[]{:S(2)}) %copy-start.4) | copy-done | bytes 262168
  5.5 0.0 copy-start.5
  5.5 0.9 %copy-done.5 = bf16[512,256]{1,0:T(8,128)(2,1)S(1)} copy-done((bf16[512,256]{1,0:T(8,128)(2,1)S(1)}, bf16[512,256]{1,0:T(8,128)(2,1)}, u32[]{:S(2)}) %copy-start.5) | copy-done | bytes 262168
  6.4 0.0 copy-start.6
  6.4 0.7 %copy-done.6 = f32[1024]{0:T(1024)S(1)} copy-done((f32[1024]{0:T(1024)S(1)}, f32[1024]{0:T(1024)}, u32[]{:S(2)}) %copy-start.6) | copy-done | bytes 4120
  7.1 38.2 %shard_map.91 = f32[128,1024]{1,0:T(8,128)S(1)} custom-call(bf16[128,1024]{1,0:T(8,128)(2,1)S(1)} %copy-done.2, bf16[128,1024]{1,0:T(8,128)(2,1)S(1)} %copy-done.3, f32[128,1024]{1,0:T(8,128)S(1)} %copy-done.1, f32[1,1024]{1,0:T(1,128)S(1)} %bitcast.1, bf16[1024,8192]{1,0:T(8,128)(2,1)} %w_hbm.1, bf16[512,256]{1,0:T(8,128)(2,1)S(1)} %copy-done.5, ...), custom_call_target="tpu_custom_call" | custom-call | flops 3221225472 | bytes 25165824 | tf_op jit(solution)/shard_map/pallas_call | solution.py:238
  45.3 0.8 %copy.11 = f32[128,1024]{1,0:T(8,128)} copy(f32[128,1024]{1,0:T(8,128)S(1)} %shard_map.91) | data formatting | bytes 1048576
Async XLA Ops:
  0.0 1.6 %copy-start = (bf16[16,256,256]{2,1,0:T(8,128)(2,1)S(1)}, bf16[16,256,256]{2,1,0:T(8,128)(2,1)}, u32[]{:S(2)}) copy-start(bf16[16,256,256]{2,1,0:T(8,128)(2,1)} %constant.9.clone.m_hbm) | copy-start | bytes 6291460
  1.6 1.0 %copy-start.1 = (f32[128,1024]{1,0:T(8,128)S(1)}, f32[128,1024]{1,0:T(8,128)}, u32[]{:S(2)}) copy-start(f32[128,1024]{1,0:T(8,128)} %h_hbm.1) | copy-start | bytes 1572868
  2.6 0.9 %copy-start.2 = (bf16[128,1024]{1,0:T(8,128)(2,1)S(1)}, bf16[128,1024]{1,0:T(8,128)(2,1)}, u32[]{:S(2)}) copy-start(bf16[128,1024]{1,0:T(8,128)(2,1)} %v_hbm.1) | copy-start | bytes 786436
  3.6 0.9 %copy-start.3 = (bf16[128,1024]{1,0:T(8,128)(2,1)S(1)}, bf16[128,1024]{1,0:T(8,128)(2,1)}, u32[]{:S(2)}) copy-start(bf16[128,1024]{1,0:T(8,128)(2,1)} %g_hbm.1) | copy-start | bytes 786436
  4.5 0.9 %copy-start.4 = (bf16[256,512]{1,0:T(8,128)(2,1)S(1)}, bf16[256,512]{1,0:T(8,128)(2,1)}, u32[]{:S(2)}) copy-start(bf16[256,512]{1,0:T(8,128)(2,1)} %constant.11.clone.f2_hbm) | copy-start | bytes 786436
  5.5 0.9 %copy-start.5 = (bf16[512,256]{1,0:T(8,128)(2,1)S(1)}, bf16[512,256]{1,0:T(8,128)(2,1)}, u32[]{:S(2)}) copy-start(bf16[512,256]{1,0:T(8,128)(2,1)} %constant.8.clone.f1_hbm) | copy-start | bytes 786436
  6.4 0.7 %copy-start.6 = (f32[1024]{0:T(1024)S(1)}, f32[1024]{0:T(1024)}, u32[]{:S(2)}) copy-start(f32[1024]{0:T(1024)} %param.12) | copy-start | bytes 12292

commit v2 on v1

--- a/solution.py
+++ b/solution.py
@@ -71,9 +71,9 @@
     return jnp.dot(left, right, preferred_element_type=jnp.float32)
 
 
-def kernel(v_hbm, g_hbm, h_hbm, bias_ref, w_hbm, f1_hbm, m_hbm, mb_hbm, f2_hbm, out_ref,
-           v, g, h, w, f1, m, mb, f2, send, recv, mid, back, bsend, brecv, gated, psend, precv, ring_s, ring_r,
-           keep, in_sem, w_sem, s_sem, r_sem, bs_sem, br_sem, ps_sem, pr_sem, rs_sem, rr_sem):
+def kernel(v_hbm, g_hbm, h_hbm, bias_hbm, w_hbm, f1_hbm, m_hbm, mb_hbm, f2_hbm, out_ref,
+           v, g, h, bias_ref, w, f1, m, mb, f2, send, recv, mid, back, bsend, brecv, gated, psend, precv, ring_s, ring_r,
+           keep, relay, in_sem, w_sem, s_sem, r_sem, bs_sem, br_sem, ps_sem, pr_sem, rs_sem, rr_sem):
     ctx, ch = lax.axis_index("ctx"), lax.axis_index("ch")
     x, y = ctx // SIDE, lax.rem(ctx, SIDE)
     z, core = ch // 2, lax.rem(ch, 2)
@@ -93,7 +93,7 @@
         pl.semaphore_signal(barrier, inc=1, device_id=device, device_id_type=MESH)
 
     loads = []
-    for i, (src, dst) in enumerate(((h_hbm, h), (v_hbm, v), (f1_hbm, f1), (m_hbm, m), (mb_hbm, mb), (f2_hbm, f2), (g_hbm, g))):
+    for i, (src, dst) in enumerate(((h_hbm, h), (v_hbm, v), (f1_hbm, f1), (m_hbm, m), (mb_hbm, mb), (f2_hbm, f2), (g_hbm, g), (bias_hbm, bias_ref))):
         load = pltpu.make_async_copy(src, dst, in_sem.at[i])
         load.start()
         loads.append(load)
@@ -154,6 +154,7 @@
         copies.append(copy)
     brecv[ctx] = bsend[ctx]
     loads[6].wait()
+    loads[7].wait()
     for copy in copies:
         copy.wait()
 
@@ -193,37 +194,42 @@
     pair = {}
     rings = {}
 
-    def pair_sum(distance, part):
-        own = project(distance, part, core)
+    def with_other(distance, part, own):
         pair[distance, part].wait_recv()
         return own + precv[2 * distance + part].astype(jnp.float32)
 
-    for part in range(2):
-        pair[2, part] = to_other(2, part)
+    for distance, part in ((2, 0), (2, 1), (1, 1), (3, 0)):
+        pair[distance, part] = to_other(distance, part)
+    for part in range(2):
+        keep[part] = project(2, part, core)
     for part, device in ((0, up), (1, down)):
-        ring_s[part] = pair_sum(2, part).astype(jnp.bfloat16)
+        ring_s[part] = with_other(2, part, keep[part]).astype(jnp.bfloat16)
         rings[part] = ring(part, device)
-    pair[1, 1], pair[3, 0] = to_other(1, 1), to_other(3, 0)
-    ring_s[2] = pair_sum(1, 1).astype(jnp.bfloat16)
-    rings[2] = ring(2, up)
-    ring_s[3] = pair_sum(3, 0).astype(jnp.bfloat16)
-    rings[3] = ring(3, down)
-    pair[1, 0], pair[3, 1] = to_other(1, 0), to_other(3, 1)
-    for i, (distance, part, device) in ((4, (1, 0, up)), (5, (3, 1, down))):
-        total = pair_sum(distance, part)
+    for distance, part in ((1, 0), (3, 1)):
+        pair[distance, part] = to_other(distance, part)
+    keep[0], keep[1] = project(1, 1, core), project(3, 0, core)
+    for i, distance, part, device in ((2, 1, 1, up), (3, 3, 0, down)):
+        ring_s[i] = with_other(distance, part, keep[i - 2]).astype(jnp.bfloat16)
+        rings[i] = ring(i, device)
+    for part in range(2):
+        pair[0, part] = to_other(0, part)
+    relay[0], relay[1] = project(1, 0, core), project(3, 1, core)
+    for part in range(2):
+        keep[part] = project(0, part, core)
+    for i, distance, part in ((0, 1, 0), (1, 3, 1)):
+        relay[i] = with_other(distance, part, relay[i])
+    for part in range(2):
+        keep[part] = with_other(0, part, keep[part])
+    for i, device in ((4, up), (5, down)):
         rings[i - 4].wait_recv()
-        ring_s[i] = (total + ring_r[i - 4].astype(jnp.float32)).astype(jnp.bfloat16)
+        ring_s[i] = (relay[i - 4] + ring_r[i - 4].astype(jnp.float32)).astype(jnp.bfloat16)
         rings[i] = ring(i, device)
-    for part in range(2):
-        pair[0, part] = to_other(0, part)
-    for part in range(2):
-        keep[part] = pair_sum(0, part)
-    for i in (2, 3):
+    for part, i in ((0, 3), (1, 2)):
         rings[i].wait_recv()
-    rings[4].wait_recv()
-    out_ref[:, 0:512] = keep[0] + (ring_r[4].astype(jnp.float32) + ring_r[3].astype(jnp.float32))
-    rings[5].wait_recv()
-    out_ref[:, 512:1024] = keep[1] + (ring_r[2].astype(jnp.float32) + ring_r[5].astype(jnp.float32))
+        keep[part] += ring_r[i].astype(jnp.float32)
+    for part, i in ((0, 4), (1, 5)):
+        rings[i].wait_recv()
+        out_ref[:, part * 512:(part + 1) * 512] = keep[part] + ring_r[i].astype(jnp.float32)
     for copy in (*pair.values(), *rings.values()):
         copy.wait_send()
 
@@ -231,19 +237,20 @@
 def on_device(keyed_values, gate_values, long_filter, skip_bias, out_weight):
     first, middle, middle_back, last = (jnp.asarray(t) for t in tables())
     bf, f32 = jnp.bfloat16, jnp.float32
-    hbm = pl.BlockSpec(memory_space=pl.ANY)
+    hbm = pl.BlockSpec(memory_space=pltpu.HBM)
     vmem = pl.BlockSpec(memory_space=pltpu.VMEM)
     dma = pltpu.SemaphoreType.DMA
     hops = len(ROUTES)
     return pl.pallas_call(
         kernel,
-        out_shape=jax.ShapeDtypeStruct((ROWS, 1024), f32),
-        in_specs=[hbm, hbm, hbm, vmem, hbm, hbm, hbm, hbm, hbm],
+        out_shape=pltpu.VMEM((ROWS, 1024), f32),
+        in_specs=[hbm, hbm, hbm, hbm, hbm, hbm, hbm, hbm, hbm],
         out_specs=vmem,
         scratch_shapes=[
             pltpu.VMEM((ROWS, 1024), bf),
             pltpu.VMEM((ROWS, 1024), bf),
             pltpu.VMEM((ROWS, 1024), f32),
+            pltpu.VMEM((1, 1024), f32),
             pltpu.VMEM((1024, 8192), bf),
             pltpu.VMEM((512, 256), bf),
             pltpu.VMEM((16, 256, 256), bf),
@@ -261,7 +268,8 @@
             pltpu.VMEM((6, ROWS, 512), bf),
             pltpu.VMEM((6, ROWS, 512), bf),
             pltpu.VMEM((2, ROWS, 512), f32),
-            dma((7,)),
+            pltpu.VMEM((2, ROWS, 512), f32),
+            dma((8,)),
             dma,
             dma((hops,)),
             dma((hops,)),
@@ -273,7 +281,7 @@
             dma((6,)),
         ],
         compiler_params=pltpu.CompilerParams(
-            collective_id=0, has_side_effects=True, vmem_limit_bytes=48 << 20),
+            collective_id=0, has_side_effects=True, vmem_limit_bytes=60 << 20),
         cost_estimate=pl.CostEstimate(flops=3 << 30, bytes_accessed=24 << 20, transcendentals=0),
     )(keyed_values, gate_values, long_filter, skip_bias.reshape(1, 1024), out_weight, first, middle, middle_back, last)
 

time: 46.4 us -> 38.3 us (0.83)
  local copies, waits for them, and re-layouts: 7.91 us -> 0.8 us
  Pallas kernels: 38.2 us -> 37.4 us
    unnamed x15 -> x1, local copies, waits for them, and re-layouts: 7.91 us -> 0.8 us
    pallas_call x1, Pallas kernels: 38.2 us -> 37.4 us  [on_device(): pl.pallas_call(kernel, out_shape=pltpu.VMEM((ROWS, 1024), f32), in_specs=...]
where the time goes in v2:
time: 38.3 us; the launch traced here: 38.2 us
  Pallas kernels  37.4 us (98%)
  local copies, waits for them, and re-layouts  0.8 us (2%)
    pallas_call x1, Pallas kernels, on_device(): pl.pallas_call(kernel, out_shape=pltpu.VMEM((ROWS, 1024), f32), in_specs=...  37.4 us
    unnamed x1, local copies, waits for them, and re-layouts  0.8 us

profile of v2, /device:TPU:1, one launch (start us, length us, event | category | flops | bytes accessed | tf_op | source)
XLA Modules:
  0.0 38.2 jit_solution(12384844201516771269)
XLA Ops:
  0.0 37.4 %shard_map.91 = f32[128,1024]{1,0:T(8,128)S(1)} custom-call(bf16[128,1024]{1,0:T(8,128)(2,1)} %v_hbm.1, bf16[128,1024]{1,0:T(8,128)(2,1)} %g_hbm.1, f32[128,1024]{1,0:T(8,128)} %h_hbm.1, f32[1,1024]{1,0:T(1,128)} %bitcast.1, bf16[1024,8192]{1,0:T(8,128)(2,1)} %w_hbm.1, bf16[512,256]{1,0:T(8,128)(2,1)} %constant.8.clone.f1_hbm, ...), custom_call_target="tpu_custom_call" | custom-call | flops 3221225472 | bytes 25165824 | tf_op jit(solution)/shard_map/pallas_call | solution.py:244
  37.4 0.8 %copy.11 = f32[128,1024]{1,0:T(8,128)} copy(f32[128,1024]{1,0:T(8,128)S(1)} %shard_map.91) | data formatting | bytes 1048576

commit v3 on v2

--- a/solution.py
+++ b/solution.py
@@ -16,6 +16,7 @@
 ROWS = 128
 LANES = 128
 HALF = 64
+SPAN = 32
 FULL = 2 * BLOCKS * ROWS
 GROUP = 16
 ROUTES = ((2, 2), (2, 1), (1, 2), (2, 3), (3, 2), (2, 0), (0, 2), (1, 1), (3, 3), (1, 3), (3, 1),
@@ -85,11 +86,13 @@
     other = (ctx, z * 2 + 1 - core)
     up = (ctx, shifted(z, 1) * 2 + core)
     down = (ctx, shifted(z, 3) * 2 + core)
+    up_crossed = (ctx, shifted(z, 1) * 2 + 1 - core)
+    down_crossed = (ctx, shifted(z, 3) * 2 + 1 - core)
 
     barrier = pltpu.get_barrier_semaphore()
     for partner in partners:
         pl.semaphore_signal(barrier, inc=1, device_id=(partner, ch), device_id_type=MESH)
-    for device in (other, up, down):
+    for device in (up_crossed, down_crossed, up, down, other):
         pl.semaphore_signal(barrier, inc=1, device_id=device, device_id_type=MESH)
 
     loads = []
@@ -109,7 +112,7 @@
         send[2 * t] = jnp.where(low, values, pltpu.roll(taps, HALF, 1)).astype(jnp.bfloat16)
         send[2 * t + 1] = jnp.where(low, pltpu.roll(values, HALF, 1), taps).astype(jnp.bfloat16)
 
-    pl.semaphore_wait(barrier, len(ROUTES) + 3)
+    pl.semaphore_wait(barrier, len(ROUTES) + 5)
     copies = []
     for i, partner in enumerate(partners):
         copy = pltpu.make_async_remote_copy(
@@ -122,97 +125,122 @@
     for copy in copies:
         copy.wait()
 
-    for k in range(ROWS // GROUP):
-        rows = slice(k * GROUP, (k + 1) * GROUP)
-        part = dot(f1[...], recv[:, rows, :].reshape(BLOCKS * GROUP, LANES))
-        mid[:, :, rows, :] = part.astype(jnp.bfloat16).reshape(16, 2, GROUP, LANES)
+    for k in range(0, ROWS // GROUP, 2):
+        both = [slice(e * GROUP, (e + 1) * GROUP) for e in (k, k + 1)]
+        pair = [recv[:, rows, :].reshape(BLOCKS * GROUP, LANES) for rows in both]
+        part = dot(f1[...], jnp.concatenate(pair, axis=1)).astype(jnp.bfloat16)
+        for e, rows in enumerate(both):
+            mid[:, :, rows, :] = part[:, e * LANES:(e + 1) * LANES].reshape(16, 2, GROUP, LANES)
     low_half = lax.broadcasted_iota(jnp.int32, (HALF, LANES), 1) < HALF
-    for s in range(16):
-        spectrum = dot(m[s], mid[s].reshape(2 * ROWS, LANES))
-        real, imag = spectrum[:ROWS], spectrum[ROWS:]
-        real2, imag2 = pltpu.roll(real, HALF, 1), pltpu.roll(imag, HALF, 1)
-        rr, ii = real * real2, imag * imag2
-        prod_real, prod_imag = rr - ii, real * imag2 + imag * real2
-        if s == 0:
-            top = lax.broadcasted_iota(jnp.int32, (ROWS, LANES), 0) == 0
-            prod_real, prod_imag = jnp.where(top, rr, prod_real), jnp.where(top, ii, prod_imag)
-        product = jnp.concatenate([prod_real, prod_imag], axis=0).astype(jnp.bfloat16)
-        turned = dot(mb[s], product)
-        for part in range(2):
-            first, second = turned[part * ROWS:part * ROWS + HALF], turned[part * ROWS + HALF:(part + 1) * ROWS]
-            back[s, part] = jnp.where(low_half, first, second).astype(jnp.bfloat16)
-    for k in range(HALF // GROUP):
-        rows = slice(k * GROUP, (k + 1) * GROUP)
-        part = dot(f2[...], back[:, :, rows, :].reshape(2 * 16 * GROUP, LANES))
-        bsend[:, rows, :] = part.astype(jnp.bfloat16).reshape(BLOCKS, GROUP, LANES)
-
-    copies = []
-    for i, partner in enumerate(partners):
-        copy = pltpu.make_async_remote_copy(
-            bsend.at[partner], brecv.at[ctx], bs_sem.at[i], br_sem.at[i], device_id=(partner, ch), device_id_type=MESH)
-        copy.start()
-        copies.append(copy)
-    brecv[ctx] = bsend[ctx]
+    for s0 in range(0, 16, 16):
+        slots = range(s0, s0 + 16)
+        spectra = [dot(m[s], mid[s].reshape(2 * ROWS, LANES)) for s in slots]
+        products = []
+        for s, spectrum in zip(slots, spectra):
+            real, imag = spectrum[:ROWS], spectrum[ROWS:]
+            real2, imag2 = pltpu.roll(real, HALF, 1), pltpu.roll(imag, HALF, 1)
+            rr, ii = real * real2, imag * imag2
+            prod_real, prod_imag = rr - ii, real * imag2 + imag * real2
+            if s == 0:
+                top = lax.broadcasted_iota(jnp.int32, (ROWS, LANES), 0) == 0
+                prod_real, prod_imag = jnp.where(top, rr, prod_real), jnp.where(top, ii, prod_imag)
+            products.append(jnp.concatenate([prod_real, prod_imag], axis=0).astype(jnp.bfloat16))
+        for s, product in zip(slots, products):
+            turned = dot(mb[s], product)
+            for part in range(2):
+                first, second = turned[part * ROWS:part * ROWS + HALF], turned[part * ROWS + HALF:(part + 1) * ROWS]
+                back[s, part] = jnp.where(low_half, first, second).astype(jnp.bfloat16)
+    returned = []
+    for q in range(2):
+        both = [slice(e * GROUP, (e + 1) * GROUP) for e in (2 * q, 2 * q + 1)]
+        pair = [back[:, :, rows, :].reshape(2 * 16 * GROUP, LANES) for rows in both]
+        part = dot(f2[...], jnp.concatenate(pair, axis=1)).astype(jnp.bfloat16)
+        for e in range(2):
+            bsend[q, :, e * GROUP:(e + 1) * GROUP, :] = part[:, e * LANES:(e + 1) * LANES].reshape(BLOCKS, GROUP, LANES)
+        copies = []
+        for i, partner in enumerate(partners):
+            copy = pltpu.make_async_remote_copy(
+                bsend.at[q, partner], brecv.at[q, ctx], bs_sem.at[q, i], br_sem.at[q, i],
+                device_id=(partner, ch), device_id_type=MESH)
+            copy.start()
+            copies.append(copy)
+        brecv[q, ctx] = bsend[q, ctx]
+        returned.append(copies)
     loads[6].wait()
     loads[7].wait()
-    for copy in copies:
-        copy.wait()
-
-    for t in range(8):
-        columns = slice(t * LANES, (t + 1) * LANES)
-        even, odd = brecv[2 * t].astype(jnp.float32), brecv[2 * t + 1].astype(jnp.float32)
-        for part in range(2):
-            rows = slice(part * HALF, (part + 1) * HALF)
-            if part == 0:
-                convolved = jnp.where(low_half, even, pltpu.roll(odd, HALF, 1))
-            else:
-                convolved = jnp.where(low_half, pltpu.roll(even, HALF, 1), odd)
-            values = v[rows, columns].astype(jnp.float32)
-            gate = g[rows, columns].astype(jnp.float32)
-            gated[rows, columns] = ((convolved + bias_ref[0:1, columns] * values) * gate).astype(jnp.bfloat16)
-
     w_load.wait()
-
-    def project(distance, part, to_core):
+    def gate(q):
+        mask = low_half[:SPAN]
+        for t in range(8):
+            columns = slice(t * LANES, (t + 1) * LANES)
+            even, odd = brecv[q, 2 * t].astype(jnp.float32), brecv[q, 2 * t + 1].astype(jnp.float32)
+            for part in range(2):
+                rows = slice(part * HALF + q * SPAN, part * HALF + (q + 1) * SPAN)
+                if part == 0:
+                    convolved = jnp.where(mask, even, pltpu.roll(odd, HALF, 1))
+                else:
+                    convolved = jnp.where(mask, pltpu.roll(even, HALF, 1), odd)
+                values = v[rows, columns].astype(jnp.float32)
+                gates = g[rows, columns].astype(jnp.float32)
+                total = ((convolved + bias_ref[0:1, columns] * values) * gates).astype(jnp.bfloat16)
+                gated[q * HALF + part * SPAN:q * HALF + (part + 1) * SPAN, columns] = total
+
+    def project(distance, part, to_core, rows=slice(0, ROWS)):
         start = (shifted(z, distance) * 2 + to_core) * 1024 + part * 512
-        return dot(gated[...], w[:, pl.ds(pl.multiple_of(start, 512), 512)])
-
-    def to_other(distance, part):
+        return dot(gated[rows, :], w[:, pl.ds(pl.multiple_of(start, 512), 512)])
+
+    first_rows, last_rows = slice(0, HALF), slice(HALF, ROWS)
+    everything = slice(0, ROWS)
+
+    def to_other(distance, part, rows=everything):
         i = 2 * distance + part
-        psend[i] = project(distance, part, 1 - core).astype(jnp.bfloat16)
+        psend[i, rows, :] = project(distance, part, 1 - core, rows).astype(jnp.bfloat16)
         copy = pltpu.make_async_remote_copy(
-            psend.at[i], precv.at[i], ps_sem.at[i], pr_sem.at[i], device_id=other, device_id_type=MESH)
+            psend.at[i, rows], precv.at[i, rows], ps_sem.at[i], pr_sem.at[i], device_id=other, device_id_type=MESH)
         copy.start()
-        return copy
-
-    def ring(i, device):
+        pair[distance, part] = copy
+
+    def with_other(distance, part, own, rows=everything):
+        pair[distance, part].wait_recv()
+        return own + precv[2 * distance + part, rows, :].astype(jnp.float32)
+
+    def ring(i, device, rows=everything):
         copy = pltpu.make_async_remote_copy(
-            ring_s.at[i], ring_r.at[i], rs_sem.at[i], rr_sem.at[i], device_id=device, device_id_type=MESH)
+            ring_s.at[i, rows], ring_r.at[i, rows], rs_sem.at[i], rr_sem.at[i], device_id=device, device_id_type=MESH)
         copy.start()
-        return copy
+        rings[i] = copy
 
     pair = {}
     rings = {}
 
-    def with_other(distance, part, own):
-        pair[distance, part].wait_recv()
-        return own + precv[2 * distance + part].astype(jnp.float32)
-
-    for distance, part in ((2, 0), (2, 1), (1, 1), (3, 0)):
-        pair[distance, part] = to_other(distance, part)
+    for copy in returned[0]:
+        copy.wait_recv()
+    gate(0)
+    for i, distance, part, to_core, device in (
+            (6, 1, 1, core, up), (7, 3, 0, core, down), (8, 1, 1, 1 - core, up_crossed), (9, 3, 0, 1 - core, down_crossed)):
+        ring_s[i, first_rows, :] = project(distance, part, to_core, first_rows).astype(jnp.bfloat16)
+        ring(i, device, first_rows)
+    for copy in returned[1]:
+        copy.wait_recv()
+    gate(1)
+    for distance, part in ((2, 0), (2, 1)):
+        to_other(distance, part)
+    for distance, part in ((1, 1), (3, 0)):
+        to_other(distance, part, last_rows)
     for part in range(2):
         keep[part] = project(2, part, core)
     for part, device in ((0, up), (1, down)):
         ring_s[part] = with_other(2, part, keep[part]).astype(jnp.bfloat16)
-        rings[part] = ring(part, device)
+        ring(part, device)
     for distance, part in ((1, 0), (3, 1)):
-        pair[distance, part] = to_other(distance, part)
-    keep[0], keep[1] = project(1, 1, core), project(3, 0, core)
+        to_other(distance, part)
+    for i, distance, part in ((0, 1, 1), (1, 3, 0)):
+        keep[i, last_rows, :] = project(distance, part, core, last_rows)
     for i, distance, part, device in ((2, 1, 1, up), (3, 3, 0, down)):
-        ring_s[i] = with_other(distance, part, keep[i - 2]).astype(jnp.bfloat16)
-        rings[i] = ring(i, device)
+        ring_s[i, last_rows, :] = with_other(distance, part, keep[i - 2, last_rows, :], last_rows).astype(jnp.bfloat16)
+        ring(i, device, last_rows)
     for part in range(2):
-        pair[0, part] = to_other(0, part)
+        to_other(0, part)
     relay[0], relay[1] = project(1, 0, core), project(3, 1, core)
     for part in range(2):
         keep[part] = project(0, part, core)
@@ -223,15 +251,22 @@
     for i, device in ((4, up), (5, down)):
         rings[i - 4].wait_recv()
         ring_s[i] = (relay[i - 4] + ring_r[i - 4].astype(jnp.float32)).astype(jnp.bfloat16)
-        rings[i] = ring(i, device)
-    for part, i in ((0, 3), (1, 2)):
-        rings[i].wait_recv()
-        keep[part] += ring_r[i].astype(jnp.float32)
+        ring(i, device)
+    for part, slots in ((0, (7, 9, 3)), (1, (6, 8, 2))):
+        for i in slots:
+            rows = last_rows if i < 4 else first_rows
+            rings[i].wait_recv()
+            keep[part, rows, :] += ring_r[i, rows, :].astype(jnp.float32)
     for part, i in ((0, 4), (1, 5)):
         rings[i].wait_recv()
-        out_ref[:, part * 512:(part + 1) * 512] = keep[part] + ring_r[i].astype(jnp.float32)
-    for copy in (*pair.values(), *rings.values()):
-        copy.wait_send()
+        total = keep[part] + ring_r[i].astype(jnp.float32)
+        for q in range(2):
+            for half in range(2):
+                token, row = half * HALF + q * SPAN, q * HALF + half * SPAN
+                out_ref[token:token + SPAN, part * 512:(part + 1) * 512] = total[row:row + SPAN]
+    for copies in (*returned, pair.values(), rings.values()):
+        for copy in copies:
+            copy.wait_send()
 
 
 def on_device(keyed_values, gate_values, long_filter, skip_bias, out_weight):
@@ -260,25 +295,25 @@
             pltpu.VMEM((BLOCKS, ROWS, LANES), bf),
             pltpu.VMEM((16, 2, ROWS, LANES), bf),
             pltpu.VMEM((16, 2, HALF, LANES), bf),
-            pltpu.VMEM((BLOCKS, HALF, LANES), bf),
-            pltpu.VMEM((BLOCKS, HALF, LANES), bf),
+            pltpu.VMEM((2, BLOCKS, SPAN, LANES), bf),
+            pltpu.VMEM((2, BLOCKS, SPAN, LANES), bf),
             pltpu.VMEM((ROWS, 1024), bf),
             pltpu.VMEM((8, ROWS, 512), bf),
             pltpu.VMEM((8, ROWS, 512), bf),
-            pltpu.VMEM((6, ROWS, 512), bf),
-            pltpu.VMEM((6, ROWS, 512), bf),
+            pltpu.VMEM((10, ROWS, 512), bf),
+            pltpu.VMEM((10, ROWS, 512), bf),
             pltpu.VMEM((2, ROWS, 512), f32),
             pltpu.VMEM((2, ROWS, 512), f32),
             dma((8,)),
             dma,
             dma((hops,)),
             dma((hops,)),
-            dma((hops,)),
-            dma((hops,)),
+            dma((2, hops)),
+            dma((2, hops)),
             dma((8,)),
             dma((8,)),
-            dma((6,)),
-            dma((6,)),
+            dma((10,)),
+            dma((10,)),
         ],
         compiler_params=pltpu.CompilerParams(
             collective_id=0, has_side_effects=True, vmem_limit_bytes=60 << 20),

time: 38.3 us -> 37 us (0.966)
  Pallas kernels: 37.4 us -> 35.8 us
    pallas_call x1, Pallas kernels: 37.4 us -> 35.8 us  [on_device(): pl.pallas_call(kernel, out_shape=pltpu.VMEM((ROWS, 1024), f32), in_specs=...]
where the time goes in v3:
time: 37 us; the launch traced here: 36.6 us
  Pallas kernels  35.8 us (97%)
  local copies, waits for them, and re-layouts  0.8 us (2%)
    pallas_call x1, Pallas kernels, on_device(): pl.pallas_call(kernel, out_shape=pltpu.VMEM((ROWS, 1024), f32), in_specs=...  35.8 us
    unnamed x1, local copies, waits for them, and re-layouts  0.8 us

profile of v3, /device:TPU:1, one launch (start us, length us, event | category | flops | bytes accessed | tf_op | source)
XLA Modules:
  0.0 36.6 jit_solution(14501027471930111681)
XLA Ops:
  0.0 35.8 %shard_map.91 = f32[128,1024]{1,0:T(8,128)S(1)} custom-call(bf16[128,1024]{1,0:T(8,128)(2,1)} %v_hbm.1, bf16[128,1024]{1,0:T(8,128)(2,1)} %g_hbm.1, f32[128,1024]{1,0:T(8,128)} %h_hbm.1, f32[1,1024]{1,0:T(1,128)} %bitcast.1, bf16[1024,8192]{1,0:T(8,128)(2,1)} %w_hbm.1, bf16[512,256]{1,0:T(8,128)(2,1)} %constant.8.clone.f1_hbm, ...), custom_call_target="tpu_custom_call" | custom-call | flops 3221225472 | bytes 25165824 | tf_op jit(solution)/shard_map/pallas_call | solution.py:279
  35.8 0.8 %copy.11 = f32[128,1024]{1,0:T(8,128)} copy(f32[128,1024]{1,0:T(8,128)S(1)} %shard_map.91) | data formatting | bytes 1048576

commit v4 on v3

--- a/solution.py
+++ b/solution.py
@@ -106,31 +106,40 @@
     low = lax.broadcasted_iota(jnp.int32, (ROWS, LANES), 1) < HALF
     loads[0].wait()
     loads[1].wait()
-    for t in range(8):
-        columns = slice(t * LANES, (t + 1) * LANES)
-        values, taps = v[:, columns].astype(jnp.float32), h[:, columns]
-        send[2 * t] = jnp.where(low, values, pltpu.roll(taps, HALF, 1)).astype(jnp.bfloat16)
-        send[2 * t + 1] = jnp.where(low, pltpu.roll(values, HALF, 1), taps).astype(jnp.bfloat16)
+    for q in range(2):
+        rows, mask = slice(q * HALF, (q + 1) * HALF), low[:HALF]
+        for t in range(8):
+            columns = slice(t * LANES, (t + 1) * LANES)
+            values, taps = v[rows, columns].astype(jnp.float32), h[rows, columns]
+            send[q, 2 * t] = jnp.where(mask, values, pltpu.roll(taps, HALF, 1)).astype(jnp.bfloat16)
+            send[q, 2 * t + 1] = jnp.where(mask, pltpu.roll(values, HALF, 1), taps).astype(jnp.bfloat16)
 
     pl.semaphore_wait(barrier, len(ROUTES) + 5)
-    copies = []
-    for i, partner in enumerate(partners):
-        copy = pltpu.make_async_remote_copy(
-            send.at[partner], recv.at[ctx], s_sem.at[i], r_sem.at[i], device_id=(partner, ch), device_id_type=MESH)
-        copy.start()
-        copies.append(copy)
-    recv[ctx] = send[ctx]
+    forth = []
+    for q in range(2):
+        copies = []
+        for i, partner in enumerate(partners):
+            copy = pltpu.make_async_remote_copy(
+                send.at[q, partner], recv.at[q, ctx], s_sem.at[q, i], r_sem.at[q, i],
+                device_id=(partner, ch), device_id_type=MESH)
+            copy.start()
+            copies.append(copy)
+        forth.append(copies)
+    for q in range(2):
+        recv[q, ctx] = send[q, ctx]
     for i in range(2, 6):
         loads[i].wait()
-    for copy in copies:
-        copy.wait()
-
-    for k in range(0, ROWS // GROUP, 2):
-        both = [slice(e * GROUP, (e + 1) * GROUP) for e in (k, k + 1)]
-        pair = [recv[:, rows, :].reshape(BLOCKS * GROUP, LANES) for rows in both]
-        part = dot(f1[...], jnp.concatenate(pair, axis=1)).astype(jnp.bfloat16)
-        for e, rows in enumerate(both):
-            mid[:, :, rows, :] = part[:, e * LANES:(e + 1) * LANES].reshape(16, 2, GROUP, LANES)
+
+    for q in range(2):
+        for copy in forth[q]:
+            copy.wait_recv()
+        for k in range(0, HALF // GROUP, 2):
+            both = [slice(e * GROUP, (e + 1) * GROUP) for e in (k, k + 1)]
+            pair = [recv[q, :, rows, :].reshape(BLOCKS * GROUP, LANES) for rows in both]
+            part = dot(f1[...], jnp.concatenate(pair, axis=1)).astype(jnp.bfloat16)
+            for e in range(2):
+                start = q * HALF + (k + e) * GROUP
+                mid[:, :, start:start + GROUP, :] = part[:, e * LANES:(e + 1) * LANES].reshape(16, 2, GROUP, LANES)
     low_half = lax.broadcasted_iota(jnp.int32, (HALF, LANES), 1) < HALF
     for s0 in range(0, 16, 16):
         slots = range(s0, s0 + 16)
@@ -264,7 +273,7 @@
             for half in range(2):
                 token, row = half * HALF + q * SPAN, q * HALF + half * SPAN
                 out_ref[token:token + SPAN, part * 512:(part + 1) * 512] = total[row:row + SPAN]
-    for copies in (*returned, pair.values(), rings.values()):
+    for copies in (*forth, *returned, pair.values(), rings.values()):
         for copy in copies:
             copy.wait_send()
 
@@ -291,8 +300,8 @@
             pltpu.VMEM((16, 256, 256), bf),
             pltpu.VMEM((16, 256, 256), bf),
             pltpu.VMEM((256, 512), bf),
-            pltpu.VMEM((BLOCKS, ROWS, LANES), bf),
-            pltpu.VMEM((BLOCKS, ROWS, LANES), bf),
+            pltpu.VMEM((2, BLOCKS, HALF, LANES), bf),
+            pltpu.VMEM((2, BLOCKS, HALF, LANES), bf),
             pltpu.VMEM((16, 2, ROWS, LANES), bf),
             pltpu.VMEM((16, 2, HALF, LANES), bf),
             pltpu.VMEM((2, BLOCKS, SPAN, LANES), bf),
@@ -306,8 +315,8 @@
             pltpu.VMEM((2, ROWS, 512), f32),
             dma((8,)),
             dma,
-            dma((hops,)),
-            dma((hops,)),
+            dma((2, hops)),
+            dma((2, hops)),
             dma((2, hops)),
             dma((2, hops)),
             dma((8,)),

time: 37 us -> 38 us (1.027)
  Pallas kernels: 35.8 us -> 36.8 us
    pallas_call x1, Pallas kernels: 35.8 us -> 36.8 us  [on_device(): pl.pallas_call(kernel, out_shape=pltpu.VMEM((ROWS, 1024), f32), in_specs=...]
where the time goes in v4:
time: 38 us; the launch traced here: 37.6 us
  Pallas kernels  36.8 us (97%)
  local copies, waits for them, and re-layouts  0.8 us (2%)
    pallas_call x1, Pallas kernels, on_device(): pl.pallas_call(kernel, out_shape=pltpu.VMEM((ROWS, 1024), f32), in_specs=...  36.8 us
    unnamed x1, local copies, waits for them, and re-layouts  0.8 us

profile of v4, /device:TPU:1, one launch (start us, length us, event | category | flops | bytes accessed | tf_op | source)
XLA Modules:
  0.0 37.6 jit_solution(5357627181827705208)
XLA Ops:
  0.0 36.8 %shard_map.91 = f32[128,1024]{1,0:T(8,128)S(1)} custom-call(bf16[128,1024]{1,0:T(8,128)(2,1)} %v_hbm.1, bf16[128,1024]{1,0:T(8,128)(2,1)} %g_hbm.1, f32[128,1024]{1,0:T(8,128)} %h_hbm.1, f32[1,1024]{1,0:T(1,128)} %bitcast.1, bf16[1024,8192]{1,0:T(8,128)(2,1)} %w_hbm.1, bf16[512,256]{1,0:T(8,128)(2,1)} %constant.8.clone.f1_hbm, ...), custom_call_target="tpu_custom_call" | custom-call | flops 3221225472 | bytes 25165824 | tf_op jit(solution)/shard_map/pallas_call | solution.py:288
  36.8 0.8 %copy.11 = f32[128,1024]{1,0:T(8,128)} copy(f32[128,1024]{1,0:T(8,128)S(1)} %shard_map.91) | data formatting | bytes 1048576

commit v5 on v3

--- a/solution.py
+++ b/solution.py
@@ -239,19 +239,19 @@
     for i, distance, part, device in ((2, 1, 1, up), (3, 3, 0, down)):
         ring_s[i, last_rows, :] = with_other(distance, part, keep[i - 2, last_rows, :], last_rows).astype(jnp.bfloat16)
         ring(i, device, last_rows)
-    for part in range(2):
-        to_other(0, part)
     relay[0], relay[1] = project(1, 0, core), project(3, 1, core)
-    for part in range(2):
-        keep[part] = project(0, part, core)
     for i, distance, part in ((0, 1, 0), (1, 3, 1)):
         relay[i] = with_other(distance, part, relay[i])
-    for part in range(2):
-        keep[part] = with_other(0, part, keep[part])
     for i, device in ((4, up), (5, down)):
         rings[i - 4].wait_recv()
         ring_s[i] = (relay[i - 4] + ring_r[i - 4].astype(jnp.float32)).astype(jnp.bfloat16)
         ring(i, device)
+    for part in range(2):
+        to_other(0, part)
+    for part in range(2):
+        keep[part] = project(0, part, core)
+    for part in range(2):
+        keep[part] = with_other(0, part, keep[part])
     for part, slots in ((0, (7, 9, 3)), (1, (6, 8, 2))):
         for i in slots:
             rows = last_rows if i < 4 else first_rows

time: 37 us -> 37 us (level)
  no operation moved by 1% of the time
where the time goes in v5:
time: 37 us; the launch traced here: 36.6 us
  Pallas kernels  35.8 us (97%)
  local copies, waits for them, and re-layouts  0.8 us (2%)
    pallas_call x1, Pallas kernels, on_device(): pl.pallas_call(kernel, out_shape=pltpu.VMEM((ROWS, 1024), f32), in_specs=...  35.8 us
    unnamed x1, local copies, waits for them, and re-layouts  0.8 us

profile of v5, /device:TPU:1, one launch (start us, length us, event | category | flops | bytes accessed | tf_op | source)
XLA Modules:
  0.0 36.6 jit_solution(16929562832211751875)
XLA Ops:
  0.0 35.8 %shard_map.91 = f32[128,1024]{1,0:T(8,128)S(1)} custom-call(bf16[128,1024]{1,0:T(8,128)(2,1)} %v_hbm.1, bf16[128,1024]{1,0:T(8,128)(2,1)} %g_hbm.1, f32[128,1024]{1,0:T(8,128)} %h_hbm.1, f32[1,1024]{1,0:T(1,128)} %bitcast.1, bf16[1024,8192]{1,0:T(8,128)(2,1)} %w_hbm.1, bf16[512,256]{1,0:T(8,128)(2,1)} %constant.8.clone.f1_hbm, ...), custom_call_target="tpu_custom_call" | custom-call | flops 3221225472 | bytes 25165824 | tf_op jit(solution)/shard_map/pallas_call | solution.py:279
  35.8 0.8 %copy.11 = f32[128,1024]{1,0:T(8,128)} copy(f32[128,1024]{1,0:T(8,128)S(1)} %shard_map.91) | data formatting | bytes 1048576
